TPU v7x, 256 devices: a whole 4x4x8 slice. The times are simulated.
256 devices in a mesh: blk: 256 (over x, y, z, core).
Axes of the slice: x: 4, y: 4, z: 8, core: 2. Of those that a mesh axis runs over, the one named last changes fastest.
Arguments:
- points: float32 [32768, 16], P('blk'), may hold values from -6 to 6, as said below
- lengthscale: float32 [16], replicated, may hold values from 1.2 to 2.5
- noise: float32 [32768], P('blk'), may hold values from 0.1 to 1
- solution: float32 [32768, 64], P('blk'), may hold values from -6 to 6
- residual: float32 [32768, 64], P('blk'), as said below
- direction: float32 [32768, 64], P('blk'), as said below
Outputs:
- new_solution: float32 [32768, 64], P('blk')
- new_residual: float32 [32768, 64], P('blk')
- new_direction: float32 [32768, 64], P('blk')
Inputs may be any that keep to these rules, and one draw needn't show every extreme that they name: `points`: real-valued, of order one. `residual`: real-valued, of order one. `direction`: real-valued, of order one.
All inputs are finite; a program needn't handle non-finite values.
Results may differ from a plain program's by a relative error of at most 0.004.
Values may be sent and summed in bfloat16 or wider, within the bound.
A program may use at most 64 MiB of HBM per device.

v0:
```python
import jax
import jax.numpy as jnp
from jax import lax
from jax.sharding import PartitionSpec as P


def kernel_tile(left, right):
    cross = lax.dot_general(
        left,
        right,
        (((1,), (1,)), ((), ())),
        precision=lax.Precision.HIGHEST,
        preferred_element_type=jnp.float32,
    )
    dist = (
        jnp.sum(left * left, axis=1)[:, None]
        + jnp.sum(right * right, axis=1)[None, :]
        - 2.0 * cross
    )
    return jnp.exp(-0.5 * dist).astype(jnp.bfloat16)


def per_device(points, lengthscale, noise, solution, residual, direction):
    scaled = points / lengthscale[None, :]
    dirb = direction.astype(jnp.bfloat16)
    every_dir = lax.all_gather(dirb, "blk", axis=0, tiled=True)
    product = jnp.dot(
        kernel_tile(scaled, lax.all_gather(scaled, "blk", axis=0, tiled=True)),
        every_dir,
        preferred_element_type=jnp.float32,
    )
    image = product + noise[:, None] * direction
    norm_old = lax.psum(jnp.sum(residual * residual, axis=0), "blk")
    curv = lax.psum(jnp.sum(direction * image, axis=0), "blk")
    alpha = norm_old / curv
    new_residual = residual - alpha[None, :] * image
    norm_new = lax.psum(jnp.sum(new_residual * new_residual, axis=0), "blk")
    new_solution = solution + alpha[None, :] * direction
    new_direction = new_residual + (norm_new / norm_old)[None, :] * direction
    return (new_solution, new_residual, new_direction)


def solution(mesh):
    placed = (P("blk", None), P(), P("blk"), P("blk", None), P("blk", None), P("blk", None))
    return jax.shard_map(
        per_device,
        mesh=mesh,
        in_specs=placed,
        out_specs=(P("blk", None), P("blk", None), P("blk", None)),
        check_vma=False,
    )
```

profile of v0, /device:TPU:1, one launch (start us, length us, event | category | flops | bytes accessed | tf_op | source)
XLA Modules:
  0.0 389.9 jit_solution(13259291570000814399)
XLA Ops:
  7.2 0.0 all-gather.3.cloned.1.call-start
  7.2 1.4 multiply_reduce_fusion.4
  8.6 0.0 all-gather.3.cloned.1.call-update
  8.6 0.0 all-gather.5.cloned.1.call-start
  8.7 1.4 convert_element_type.7
  10.0 0.0 all-gather.5.cloned.1.call-update
  10.1 0.9 multiply_reduce_fusion.3
  10.9 110.0 %all-gather.3.cloned.1.call-done = f32[32768,16]{0,1:T(8,128)} async-done(((f32[128,16]{0,1:T(8,128)}), f32[32768,16]{0,1:T(8,128)}) %all-gather.3.cloned.1.call-update) | async-done | bytes 2097168 | tf_op jit(solution)/shard_map/all_gather | solution.py:28
  120.9 2.0 multiply_reduce_fusion
  122.9 0.0 copy-start
  122.9 0.0 copy-start.4
  122.9 19.3 %fusion.3 = bf16[128,32768]{1,0:T(8,128)(2,1)} fusion(f32[128,16]{0,1:T(8,128)} %get-tuple-element.8, f32[32768,16]{0,1:T(8,128)} %all-gather.3.cloned.1.call-done, f32[32768]{0:T(1024)S(1)} %multiply_reduce_fusion, f32[128]{0:T(128)S(1)} %get-tuple-element.7), kind=kOutput, calls=%fused_computation.4 | convolution fusion | flops 826277888 | bytes 10625536 | tf_op jit(solution)/shard_map/dot_general | solution.py:8
  142.3 0.0 copy-start.2
  142.3 0.0 copy-start.3
  142.3 82.5 %all-gather.5.cloned.1.call-done = bf16[32768,64]{0,1:T(8,128)(2,1)} async-done(((bf16[128,64]{0,1:T(8,128)(2,1)}), bf16[32768,64]{0,1:T(8,128)(2,1)}) %all-gather.5.cloned.1.call-update) | async-done | bytes 4194320 | tf_op jit(solution)/shard_map/all_gather | solution.py:26
  224.8 0.0 copy-done
  224.8 0.0 copy-done.4
  224.8 7.7 %multiply_reduce_fusion.2 = (f32[64]{0:T(128)S(1)}, f32[128,64]{0,1:T(8,128)S(1)}) fusion(f32[128,64]{0,1:T(8,128)S(1)} %copy-done, f32[128]{0:T(128)S(1)} %copy-done.4, bf16[128,32768]{1,0:T(8,128)(2,1)} %fusion.3, bf16[32768,64]{0,1:T(8,128)(2,1)} %all-gather.5.cloned.1.call-done), kind=kOutput, calls=%fused_computation.11 | convolution fusion | flops 536903616 | bytes 12649216 | tf_op jit(solution)/shard_map/dot_general | solution.py:27
  232.4 77.3 %all-reduce = (f32[64]{0:T(128)S(1)}, f32[64]{0:T(128)S(1)}) all-reduce(f32[64]{0:T(128)S(1)} %multiply_reduce_fusion.3, f32[64]{0:T(128)S(1)} %get-tuple-element.11), channel_id=1, replica_groups=mesh['blk'=256] {'blk'}, use_global_device_ids=true, to_apply=%region_1.0 | all-reduce | flops 128 | bytes 1024 | tf_op jit(solution)/shard_map/psum | solution.py:33
  309.8 0.0 copy-done.2
  309.8 0.2 multiply_reduce_fusion.1
  310.0 0.0 copy-start.1
  310.0 72.4 %psum.23 = f32[64]{0:T(128)S(1)} all-reduce(f32[64]{0:T(128)S(1)} %get-tuple-element.5), channel_id=1, replica_groups=mesh['blk'=256] {'blk'}, use_global_device_ids=true, to_apply=%region_7.0 | all-reduce | flops 64 | bytes 512 | tf_op jit(solution)/shard_map/psum | solution.py:37
  382.4 0.0 copy-done.3
  382.4 0.7 multiply_add_fusion
  383.1 0.0 copy-done.1
  (2 shorter events, 0.0 us)
Async XLA Ops:
  7.2 113.8 %all-gather.3.cloned.1.call-start = ((), (), s32[]{:S(2)}) async-start(), calls=%async_computation | async-start | bytes 2105344 | tf_op jit(solution)/shard_map/all_gather | solution.py:28
  8.6 216.1 %all-gather.5.cloned.1.call-start = ((), (), s32[]{:S(2)}) async-start(), calls=%async_computation.1 | async-start | bytes 4210688 | tf_op jit(solution)/shard_map/all_gather | solution.py:26
  122.9 101.9 %copy-start = (f32[128,64]{0,1:T(8,128)S(1)}, f32[128,64]{0,1:T(8,128)}, u32[]{:S(2)}) copy-start(f32[128,64]{0,1:T(8,128)} %param.11) | copy-start | bytes 98308
  122.9 101.8 %copy-start.4 = (f32[128]{0:T(128)S(1)}, f32[128]{0:T(128)}, u32[]{:S(2)}) copy-start(f32[128]{0:T(128)} %param.8) | copy-start | bytes 1540
  142.3 167.5 %copy-start.2 = (f32[128,64]{0,1:T(8,128)S(1)}, f32[128,64]{0,1:T(8,128)}, u32[]{:S(2)}) copy-start(f32[128,64]{0,1:T(8,128)} %param.10) | copy-start | bytes 98308
  142.3 240.1 %copy-start.3 = (f32[128,64]{0,1:T(8,128)S(1)}, f32[128,64]{0,1:T(8,128)}, u32[]{:S(2)}) copy-start(f32[128,64]{0,1:T(8,128)} %param.9) | copy-start | bytes 98308
  310.0 73.1 %copy-start.1 = (f32[128,64]{0,1:T(8,128)}, f32[128,64]{0,1:T(8,128)S(1)}, u32[]{:S(2)}) copy-start(f32[128,64]{0,1:T(8,128)S(1)} %get-tuple-element.6) | copy-start | bytes 98308
Sparse Core Ops, SparseCore 0:
  12.4 108.5 all-gather.2
  125.3 99.4 all-gather.4
where the time goes:
time: 390 us
  waiting for transfers between devices  193 us (49%)
  blocking collectives  150 us (38%)
  matrix products  27 us (7%)
  between operations  14.1 us (4%)
  other arithmetic  6.46 us (2%)
    all_gather x1, waiting for transfers between devices, per_device(): lax.all_gather(scaled, 'blk', axis=0, tiled=True)  110 us
    all_gather x1, waiting for transfers between devices, per_device(): every_dir = lax.all_gather(dirb, 'blk', axis=0, tiled=True)  82.5 us
    psum x1, blocking collectives, per_device(): norm_old = lax.psum(jnp.sum(residual * residual, axis=0), 'blk')  77.3 us
    psum x1, blocking collectives, per_device(): norm_new = lax.psum(jnp.sum(new_residual * new_residual, axis=0), 'blk')  72.4 us
    dot_general x1, matrix products, kernel_tile(): lax.dot_general(left, right, (((1,), (1,)), ((), ())), precision=lax.Prec...  19.3 us
  transfers between devices with their start and end apart: 2, of which 2 were waited for; matrix products, arithmetic and copies ran while one was open for 6% of the time, Pallas kernels for 0%

commit v1 on v0

v1 whole, which is shorter than its diff:
```python
import functools
import math

import jax
import jax.numpy as jnp
from jax import lax
from jax.experimental import pallas as pl
from jax.experimental.pallas import tpu as pltpu
from jax.sharding import PartitionSpec as P

ROWS = 128
FEATURES = 16
PROBES = 64
X, Y, Z = 4, 4, 8
PLANE = X * Y
MSG = 2 * FEATURES + PROBES
FEAT = 5 * FEATURES
GROUP = 4
ROOT_LOG2E = math.sqrt(math.log2(math.e))
MESH = pl.DeviceIdType.MESH
BF = jnp.bfloat16
F32 = jnp.float32


def norm_rows(hi, lo, own_first):
    s = hi.astype(F32) + lo.astype(F32)
    n = -0.5 * jnp.sum(s * s, axis=0, keepdims=True)
    n1 = n.astype(BF).astype(F32)
    n2 = (n - n1).astype(BF).astype(F32)
    n3 = n - n1 - n2
    row = lax.broadcasted_iota(jnp.int32, (FEATURES, hi.shape[1]), 0)
    at = 0 if own_first else 3
    out = jnp.where((row >= 3 - at) & (row < 6 - at), 1.0, 0.0)
    for step, part in enumerate((n1, n2, n3)):
        out = jnp.where(row == at + step, part, out)
    return out.astype(BF)


def row_features(hi, lo):
    return jnp.concatenate([hi, hi, lo, lo, norm_rows(hi, lo, True)], axis=0)


def col_features(hi, lo):
    return jnp.concatenate([hi, lo, hi, lo, norm_rows(hi, lo, False)], axis=0)


def total_lanes(v):
    return jnp.sum(v, axis=1, keepdims=True)


def pack(lane, cols, first, out):
    for t in range(PROBES // 8):
        out = jnp.where(lane == first + t, cols[8 * t : 8 * t + 8], out)
    return out


def body(
    pts, ls, noise, sol, res, dirn,
    o_sol, o_res, o_dir,
    v_pts, v_ls, v_noise, v_sol, v_res, v_dir,
    rowbuf, colbuf, feat, acc, part, ar1, ar2,
    in_sem, row_s, row_r, col_s, col_r, sib_s, sib_r, rs_s, rs_r, a1_s, a1_r, a2_s, a2_r,
):
    me = lax.axis_index("blk")
    c = lax.rem(me, 2)
    z = lax.rem(me // 2, Z)
    y = lax.rem(me // (2 * Z), Y)
    x = me // (2 * Z * Y)

    def at(dx, dy, dz, dc):
        cc = c if dc == 0 else 1 - c
        zz = lax.rem(z + dz, Z)
        yy = lax.rem(y + dy, Y)
        xx = lax.rem(x + dx, X)
        return ((xx * Y + yy) * Z + zz) * 2 + cc

    plane = [(k // Y, k % Y) for k in range(PLANE)]
    column = [(k % Z, k // Z) for k in range(2 * Z)]
    plane_id = [at(dx, dy, 0, 0) for dx, dy in plane]
    column_id = [at(0, 0, dz, dc) for dz, dc in column]

    def remote(src, dst, s, r, dev):
        return pltpu.make_async_remote_copy(
            src_ref=src, dst_ref=dst, send_sem=s, recv_sem=r, device_id=(dev,), device_id_type=MESH
        )

    loads = [
        pltpu.make_async_copy(src, dst, in_sem.at[i])
        for i, (src, dst) in enumerate(
            ((pts, v_pts), (ls, v_ls), (dirn, v_dir), (res, v_res), (noise, v_noise), (sol, v_sol))
        )
    ]
    for load in loads:
        load.start()
    barrier = pltpu.get_barrier_semaphore()
    for dev in plane_id[1:] + column_id[1:]:
        pl.semaphore_signal(barrier, inc=1, device_id=(dev,), device_id_type=MESH)

    loads[0].wait()
    loads[1].wait()
    eye = lax.broadcasted_iota(jnp.int32, (FEATURES, FEATURES), 0) == lax.broadcasted_iota(
        jnp.int32, (FEATURES, FEATURES), 1
    )
    scale = total_lanes(jnp.where(eye, jnp.broadcast_to(v_ls[...], (FEATURES, FEATURES)), 0.0))
    scaled = v_pts[...] / scale * ROOT_LOG2E
    hi = scaled.astype(BF)
    lo = (scaled - hi.astype(F32)).astype(BF)
    rowbuf[0, 0:FEATURES] = hi
    rowbuf[0, FEATURES : 2 * FEATURES] = lo
    colbuf[0, 0, 0:FEATURES] = hi
    colbuf[0, 0, FEATURES : 2 * FEATURES] = lo
    loads[2].wait()
    colbuf[0, 0, 2 * FEATURES : MSG] = v_dir[...].astype(BF)

    pl.semaphore_wait(barrier, 30)
    rows = [
        remote(rowbuf.at[0], rowbuf.at[Z - k], row_s.at[k], row_r.at[Z - k], column_id[k])
        for k in range(1, Z)
    ]
    for copy in rows:
        copy.start()
    cols = []
    for k in range(1, PLANE):
        dx, dy = plane[k]
        slot = ((X - dx) % X) * Y + (Y - dy) % Y
        cols.append(
            remote(colbuf.at[0, 0], colbuf.at[0, slot], col_s.at[k], col_r.at[slot], plane_id[k])
        )
    for copy in cols:
        copy.start()

    for load in loads[3:]:
        load.wait()
    lane = lax.broadcasted_iota(jnp.int32, (8, 128), 1)
    sums = pack(lane, total_lanes(v_res[...] * v_res[...]), 0, jnp.zeros((8, 128), F32))

    feat[:, 0:ROWS] = row_features(rowbuf[0, 0:FEATURES], rowbuf[0, FEATURES : 2 * FEATURES])
    for k in range(1, Z):
        remote(rowbuf.at[0], rowbuf.at[k], row_s.at[k], row_r.at[k], column_id[k]).wait_recv()
    for k in range(1, Z):
        feat[:, k * ROWS : (k + 1) * ROWS] = row_features(
            rowbuf[k, 0:FEATURES], rowbuf[k, FEATURES : 2 * FEATURES]
        )

    def product(half, first, rows_at, rows_n):
        blocks = range(first, first + GROUP)
        b = jnp.concatenate(
            [
                col_features(colbuf[half, j, 0:FEATURES], colbuf[half, j, FEATURES : 2 * FEATURES])
                for j in blocks
            ],
            axis=1,
        )
        d = jnp.concatenate([colbuf[half, j, 2 * FEATURES : MSG] for j in blocks], axis=1)
        s = lax.dot_general(
            b, feat[:, rows_at : rows_at + rows_n], (((0,), (0,)), ((), ())), preferred_element_type=F32
        )
        return jnp.dot(d, jnp.exp2(s).astype(BF), preferred_element_type=F32)

    forwards = []
    for g in range(PLANE // GROUP):
        for slot in range(g * GROUP, (g + 1) * GROUP):
            if slot:
                remote(
                    colbuf.at[0, 0], colbuf.at[0, slot], col_s.at[slot], col_r.at[slot], plane_id[slot]
                ).wait_recv()
        part_of = pl.ds(g * GROUP, GROUP)
        forward = remote(
            colbuf.at[0, part_of], colbuf.at[1, part_of], sib_s.at[g], sib_r.at[g], column_id[Z]
        )
        forward.start()
        forwards.append(forward)
        q = product(0, g * GROUP, 0, Z * ROWS)
        if g == 0:
            acc[...] = q
        else:
            acc[...] += q
    for g in range(PLANE // GROUP):
        forwards[g].wait_recv()
        acc[...] += product(1, g * GROUP, 0, Z * ROWS)

    for k in range(1, Z):
        part[k] = acc[:, k * ROWS : (k + 1) * ROWS]
    homes = [
        remote(part.at[k], part.at[2 * Z - k], rs_s.at[k], rs_r.at[Z - k], column_id[k])
        for k in range(1, Z)
    ]
    for copy in homes:
        copy.start()
    image = acc[:, 0:ROWS] + v_noise[...] * v_dir[...]
    for k in range(1, Z):
        remote(part.at[k], part.at[Z + k], rs_s.at[k], rs_r.at[k], column_id[k]).wait_recv()
    for k in range(1, Z):
        image += part[Z + k]

    sums = pack(lane, total_lanes(v_dir[...] * image), 8, sums)
    sums = pack(lane, total_lanes(v_res[...] * image), 16, sums)
    sums = pack(lane, total_lanes(image * image), 24, sums)

    ar1[0] = sums
    firsts = []
    for k in range(1, 2 * Z):
        dz, dc = column[k]
        slot = (Z - dz) % Z + dc * Z
        firsts.append(remote(ar1.at[0], ar1.at[slot], a1_s.at[k], a1_r.at[slot], column_id[k]))
    for copy in firsts:
        copy.start()
    for k in range(1, 2 * Z):
        remote(ar1.at[0], ar1.at[k], a1_s.at[k], a1_r.at[k], column_id[k]).wait_recv()
    ar2[0] = jnp.sum(ar1[...], axis=0)
    seconds = []
    for k in range(1, PLANE):
        dx, dy = plane[k]
        slot = ((X - dx) % X) * Y + (Y - dy) % Y
        seconds.append(remote(ar2.at[0], ar2.at[slot], a2_s.at[k], a2_r.at[slot], plane_id[k]))
    for copy in seconds:
        copy.start()
    for k in range(1, PLANE):
        remote(ar2.at[0], ar2.at[k], a2_s.at[k], a2_r.at[k], plane_id[k]).wait_recv()
    total = jnp.sum(ar2[...], axis=0)

    alpha = total / pltpu.roll(total, 120, 1)
    change = alpha * (alpha * pltpu.roll(total, 104, 1) - 2.0 * pltpu.roll(total, 112, 1))
    beta = (total + change) / total
    for t in range(PROBES // 8):
        at8 = slice(8 * t, 8 * t + 8)
        a = alpha[:, t : t + 1]
        new = v_res[at8] - a * image[at8]
        o_res[at8] = new
        o_sol[at8] = v_sol[at8] + a * v_dir[at8]
        o_dir[at8] = new + beta[:, t : t + 1] * v_dir[at8]

    for copy in rows + cols + forwards + homes + firsts + seconds:
        copy.wait_send()


def per_device(points, lengthscale, noise, solution, residual, direction):
    sems = pltpu.SemaphoreType.DMA
    out = jax.ShapeDtypeStruct((PROBES, ROWS), F32)
    hbm = pl.BlockSpec(memory_space=pltpu.HBM)
    vmem = pl.BlockSpec(memory_space=pltpu.VMEM)
    outs = pl.pallas_call(
        body,
        out_shape=(out, out, out),
        in_specs=[hbm] * 6,
        out_specs=(vmem, vmem, vmem),
        scratch_shapes=[
            pltpu.VMEM((FEATURES, ROWS), F32),
            pltpu.VMEM((1, FEATURES), F32),
            pltpu.VMEM((1, ROWS), F32),
            pltpu.VMEM((PROBES, ROWS), F32),
            pltpu.VMEM((PROBES, ROWS), F32),
            pltpu.VMEM((PROBES, ROWS), F32),
            pltpu.VMEM((Z, 2 * FEATURES, ROWS), BF),
            pltpu.VMEM((2, PLANE, MSG, ROWS), BF),
            pltpu.VMEM((FEAT, Z * ROWS), BF),
            pltpu.VMEM((PROBES, Z * ROWS), F32),
            pltpu.VMEM((2 * Z, PROBES, ROWS), F32),
            pltpu.VMEM((2 * Z, 8, 128), F32),
            pltpu.VMEM((PLANE, 8, 128), F32),
            sems((6,)),
            sems((Z,)), sems((Z,)),
            sems((PLANE,)), sems((PLANE,)),
            sems((PLANE // GROUP,)), sems((PLANE // GROUP,)),
            sems((Z,)), sems((Z,)),
            sems((2 * Z,)), sems((2 * Z,)),
            sems((PLANE,)), sems((PLANE,)),
        ],
        compiler_params=pltpu.CompilerParams(
            collective_id=0, has_side_effects=True, vmem_limit_bytes=32 << 20
        ),
    )(
        points.T, lengthscale[None, :], noise[None, :], solution.T, residual.T, direction.T
    )
    return tuple(o.T for o in outs)


def solution(mesh):
    placed = (P("blk", None), P(), P("blk"), P("blk", None), P("blk", None), P("blk", None))
    return jax.shard_map(
        per_device,
        mesh=mesh,
        in_specs=placed,
        out_specs=(P("blk", None), P("blk", None), P("blk", None)),
        check_vma=False,
    )
```

time: 390 us -> 47 us (0.12)
  waiting for transfers between devices: 193 us -> 0 us
  blocking collectives: 150 us -> 0 us
  Pallas kernels: 0 us -> 41.2 us
  matrix products: 27 us -> 0 us
  between operations: 14.1 us -> 0.67 us
  other arithmetic: 6.46 us -> 0 us
  local copies, waits for them, and re-layouts: 0.03 us -> 4.8 us
    all_gather x2 -> x0, waiting for transfers between devices: 193 us -> none  [the longest x1 110 us: per_device(): lax.all_gather(scaled, 'blk', axis=0, tiled=True)]
    psum x2 -> x0, blocking collectives: 150 us -> none  [the longest x1 77.3 us: per_device(): norm_old = lax.psum(jnp.sum(residual * residual, axis=0), 'blk')]
    pallas_call x0 -> x1, Pallas kernels: none -> 41.2 us  [per_device(): pl.pallas_call(body, out_shape=(out, out, out), in_specs=[hbm] * 6, out_s...]
    dot_general x2 -> x0, matrix products: 27 us -> none  [the longest x1 19.3 us: kernel_tile(): lax.dot_general(left, right, (((1,), (1,)), ((), ())), precision=lax.Prec...]
    unnamed x10 -> x15, local copies, waits for them, and re-layouts: 0.03 us -> 4.8 us
    reduce_sum x4 -> x0, other arithmetic: 4.37 us -> none  [the longest x1 1.95 us: kernel_tile(): jnp.sum(right * right, axis=1)[None, :]]
  transfers between devices with their start and end apart: 2 -> 0, of which waited for: 2 -> 0; matrix products, arithmetic and copies ran while one was open for 6% -> 0% of each run, Pallas kernels for 0% -> 0%
where the time goes in v1:
time: 47 us; the launch traced here: 46.6 us
  Pallas kernels  41.2 us (88%)
  local copies, waits for them, and re-layouts  4.8 us (10%)
  between operations  0.67 us (1%)
    pallas_call x1, Pallas kernels, per_device(): pl.pallas_call(body, out_shape=(out, out, out), in_specs=[hbm] * 6, out_s...  41.2 us
    unnamed x15, local copies, waits for them, and re-layouts  4.8 us

profile of v1, /device:TPU:1, one launch (start us, length us, event | category | flops | bytes accessed | tf_op | source)
XLA Modules:
  0.0 46.6 jit_solution(4031081893836982794)
XLA Ops:
  0.6 0.0 copy-start.3
  0.6 0.0 copy-start.4
  0.7 0.0 copy-start.5
  0.7 0.7 %copy-done.3 = f32[128,16]{0,1:T(8,128)S(1)} copy-done((f32[128,16]{0,1:T(8,128)S(1)}, f32[128,16]{0,1:T(8,128)}, u32[]{:S(2)}) %copy-start.3) | copy-done | bytes 8216
  1.3 0.0 copy-done.4
  1.3 0.0 copy-done.5
  1.3 0.0 copy-start
  1.3 0.8 %copy-done = f32[128,64]{0,1:T(8,128)S(1)} copy-done((f32[128,64]{0,1:T(8,128)S(1)}, f32[128,64]{0,1:T(8,128)}, u32[]{:S(2)}) %copy-start) | copy-done | bytes 32792
  2.1 0.0 copy-start.1
  2.1 0.8 %copy-done.1 = f32[128,64]{0,1:T(8,128)S(1)} copy-done((f32[128,64]{0,1:T(8,128)S(1)}, f32[128,64]{0,1:T(8,128)}, u32[]{:S(2)}) %copy-start.1) | copy-done | bytes 32792
  2.9 0.0 copy-start.2
  2.9 0.8 %copy-done.2 = f32[128,64]{0,1:T(8,128)S(1)} copy-done((f32[128,64]{0,1:T(8,128)S(1)}, f32[128,64]{0,1:T(8,128)}, u32[]{:S(2)}) %copy-start.2) | copy-done | bytes 32792
  3.6 41.2 %shard_map.85 = (f32[64,128]{1,0:T(8,128)S(1)}, f32[64,128]{1,0:T(8,128)S(1)}, f32[64,128]{1,0:T(8,128)S(1)}) custom-call(f32[16,128]{1,0:T(8,128)S(1)} %bitcast.15, f32[1,16]{1,0:T(1,128)S(1)} %bitcast.16, f32[1,128]{1,0:T(1,128)S(1)} %bitcast.17, f32[64,128]{1,0:T(8,128)S(1)} %bitcast.9, f32[64,128]{1,0:T(8,128)S(1)} %bitcast.10, f32[64,128]{1,0:T(8,128)S(1)} %bitcast.11), custom_call_target="tpu_custom_call" | custom-call | tf_op jit(solution)/shard_map/pallas_call | solution.py:242
  44.8 0.6 %copy.12 = f32[128,64]{0,1:T(8,128)} copy(f32[128,64]{0,1:T(8,128)S(1)} %bitcast.14) | data formatting | bytes 65536
  45.4 0.6 %copy.13 = f32[128,64]{0,1:T(8,128)} copy(f32[128,64]{0,1:T(8,128)S(1)} %bitcast.13) | data formatting | bytes 65536
  46.0 0.6 %copy.14 = f32[128,64]{0,1:T(8,128)} copy(f32[128,64]{0,1:T(8,128)S(1)} %bitcast.12) | data formatting | bytes 65536
Async XLA Ops:
  0.6 0.7 %copy-start.3 = (f32[128,16]{0,1:T(8,128)S(1)}, f32[128,16]{0,1:T(8,128)}, u32[]{:S(2)}) copy-start(f32[128,16]{0,1:T(8,128)} %param.6) | copy-start | bytes 24580
  0.6 0.7 %copy-start.4 = (f32[16]{0:T(128)S(1)}, f32[16]{0:T(128)}, u32[]{:S(2)}) copy-start(f32[16]{0:T(128)} %param.7) | copy-start | bytes 196
  0.7 0.7 %copy-start.5 = (f32[128]{0:T(128)S(1)}, f32[128]{0:T(128)}, u32[]{:S(2)}) copy-start(f32[128]{0:T(128)} %param.8) | copy-start | bytes 1540
  1.3 0.8 %copy-start = (f32[128,64]{0,1:T(8,128)S(1)}, f32[128,64]{0,1:T(8,128)}, u32[]{:S(2)}) copy-start(f32[128,64]{0,1:T(8,128)} %param.9) | copy-start | bytes 98308
  2.1 0.8 %copy-start.1 = (f32[128,64]{0,1:T(8,128)S(1)}, f32[128,64]{0,1:T(8,128)}, u32[]{:S(2)}) copy-start(f32[128,64]{0,1:T(8,128)} %param.10) | copy-start | bytes 98308
  2.9 0.8 %copy-start.2 = (f32[128,64]{0,1:T(8,128)S(1)}, f32[128,64]{0,1:T(8,128)}, u32[]{:S(2)}) copy-start(f32[128,64]{0,1:T(8,128)} %param.11) | copy-start | bytes 98308

commit v2 on v1

v2 whole, which is shorter than its diff:
```python
import functools
import math

import jax
import jax.numpy as jnp
from jax import lax
from jax.experimental import pallas as pl
from jax.experimental.pallas import tpu as pltpu
from jax.sharding import PartitionSpec as P

ROWS = 128
FEATURES = 16
PROBES = 64
X, Y, Z = 4, 4, 8
PLANE = X * Y
MSG = 2 * FEATURES + PROBES
FEAT = 5 * FEATURES
GROUP = 4
ROOT_LOG2E = math.sqrt(math.log2(math.e))
MESH = pl.DeviceIdType.MESH
BF = jnp.bfloat16
F32 = jnp.float32


def norm_rows(hi, lo, own_first):
    s = hi.astype(F32) + lo.astype(F32)
    n = -0.5 * jnp.sum(s * s, axis=0, keepdims=True)
    n1 = n.astype(BF).astype(F32)
    n2 = (n - n1).astype(BF).astype(F32)
    n3 = n - n1 - n2
    row = lax.broadcasted_iota(jnp.int32, (FEATURES, hi.shape[1]), 0)
    at = 0 if own_first else 3
    out = jnp.where((row >= 3 - at) & (row < 6 - at), 1.0, 0.0)
    for step, part in enumerate((n1, n2, n3)):
        out = jnp.where(row == at + step, part, out)
    return out.astype(BF)


def row_features(hi, lo):
    return jnp.concatenate([hi, hi, lo, lo, norm_rows(hi, lo, True)], axis=0)


def col_features(hi, lo):
    return jnp.concatenate([hi, lo, hi, lo, norm_rows(hi, lo, False)], axis=0)


def total_lanes(v):
    return jnp.sum(v, axis=1, keepdims=True)


def pack(lane, cols, first, out):
    for t in range(PROBES // 8):
        out = jnp.where(lane == first + t, cols[8 * t : 8 * t + 8], out)
    return out


def body(
    pts, ls, noise, res, dirn,
    o_image, o_alpha, o_beta,
    v_pts, v_ls, v_noise, v_res, v_dir,
    rowbuf, colbuf, feat, acc, part, ar1, ar2,
    in_sem, row_s, row_r, col_s, col_r, sib_s, sib_r, rs_s, rs_r, a1_s, a1_r, a2_s, a2_r,
):
    me = lax.axis_index("blk")
    c = lax.rem(me, 2)
    z = lax.rem(me // 2, Z)
    y = lax.rem(me // (2 * Z), Y)
    x = me // (2 * Z * Y)

    def at(dx, dy, dz, dc):
        cc = c if dc == 0 else 1 - c
        zz = lax.rem(z + dz, Z)
        yy = lax.rem(y + dy, Y)
        xx = lax.rem(x + dx, X)
        return ((xx * Y + yy) * Z + zz) * 2 + cc

    def hops(dx, dy, dz):
        return min(dx, X - dx) + min(dy, Y - dy) + min(dz, Z - dz)

    plane = sorted(((k // Y, k % Y) for k in range(PLANE)), key=lambda o: hops(o[0], o[1], 0))
    ring = sorted(range(Z), key=lambda dz: hops(0, 0, dz))
    column = sorted(((dz, dc) for dz in range(Z) for dc in range(2)), key=lambda o: 2 * hops(0, 0, o[0]) + o[1])
    plane_id = [at(dx, dy, 0, 0) for dx, dy in plane]
    ring_id = [at(0, 0, dz, 0) for dz in ring]
    column_id = [at(0, 0, dz, dc) for dz, dc in column]
    sibling = at(0, 0, 0, 1)
    plane_back = [plane.index(((X - dx) % X, (Y - dy) % Y)) for dx, dy in plane]
    ring_back = [ring.index((Z - dz) % Z) for dz in ring]
    column_back = [column.index(((Z - dz) % Z, dc)) for dz, dc in column]

    def remote(src, dst, s, r, dev):
        return pltpu.make_async_remote_copy(
            src_ref=src, dst_ref=dst, send_sem=s, recv_sem=r, device_id=(dev,), device_id_type=MESH
        )

    loads = [
        pltpu.make_async_copy(src, dst, in_sem.at[i])
        for i, (src, dst) in enumerate(
            ((pts, v_pts), (ls, v_ls), (dirn, v_dir), (res, v_res), (noise, v_noise))
        )
    ]
    for load in loads:
        load.start()
    barrier = pltpu.get_barrier_semaphore()
    for dev in ring_id[:0:-1] + plane_id[:0:-1] + [sibling]:
        pl.semaphore_signal(barrier, inc=1, device_id=(dev,), device_id_type=MESH)

    loads[0].wait()
    loads[1].wait()
    eye = lax.broadcasted_iota(jnp.int32, (FEATURES, FEATURES), 0) == lax.broadcasted_iota(
        jnp.int32, (FEATURES, FEATURES), 1
    )
    scale = total_lanes(jnp.where(eye, jnp.broadcast_to(v_ls[...], (FEATURES, FEATURES)), 0.0))
    scaled = v_pts[...] / scale * ROOT_LOG2E
    hi = scaled.astype(BF)
    lo = (scaled - hi.astype(F32)).astype(BF)
    rowbuf[0, 0:FEATURES] = hi
    rowbuf[0, FEATURES : 2 * FEATURES] = lo
    colbuf[0, 0, 0:FEATURES] = hi
    colbuf[0, 0, FEATURES : 2 * FEATURES] = lo
    loads[2].wait()
    colbuf[0, 0, 2 * FEATURES : MSG] = v_dir[...].astype(BF)

    pl.semaphore_wait(barrier, PLANE + Z - 1)
    rows = [
        remote(rowbuf.at[0], rowbuf.at[ring_back[k]], row_s.at[k], row_r.at[ring_back[k]], ring_id[k])
        for k in range(Z - 1, 0, -1)
    ]
    cols = [
        remote(
            colbuf.at[0, 0], colbuf.at[0, plane_back[k]], col_s.at[k], col_r.at[plane_back[k]], plane_id[k]
        )
        for k in range(PLANE - 1, 0, -1)
    ]
    for copy in rows + cols:
        copy.start()

    for load in loads[3:]:
        load.wait()
    lane = lax.broadcasted_iota(jnp.int32, (8, 128), 1)
    sums = pack(lane, total_lanes(v_res[...] * v_res[...]), 0, jnp.zeros((8, 128), F32))

    def rows_in(first, last):
        for k in range(max(first, 1), last):
            remote(rowbuf.at[0], rowbuf.at[k], row_s.at[k], row_r.at[k], ring_id[k]).wait_recv()
        for k in range(first, last):
            feat[:, k * ROWS : (k + 1) * ROWS] = row_features(
                rowbuf[k, 0:FEATURES], rowbuf[k, FEATURES : 2 * FEATURES]
            )

    def cols_in(g):
        for k in range(max(g * GROUP, 1), (g + 1) * GROUP):
            remote(colbuf.at[0, 0], colbuf.at[0, k], col_s.at[k], col_r.at[k], plane_id[k]).wait_recv()
        here = pl.ds(g * GROUP, GROUP)
        copy = remote(colbuf.at[0, here], colbuf.at[1, here], sib_s.at[g], sib_r.at[g], sibling)
        copy.start()
        return copy

    def product(half, first, rows_at, rows_n):
        blocks = range(first, first + GROUP)
        b = jnp.concatenate(
            [
                col_features(colbuf[half, j, 0:FEATURES], colbuf[half, j, FEATURES : 2 * FEATURES])
                for j in blocks
            ],
            axis=1,
        )
        d = jnp.concatenate([colbuf[half, j, 2 * FEATURES : MSG] for j in blocks], axis=1)
        s = lax.dot_general(
            b, feat[:, rows_at : rows_at + rows_n], (((0,), (0,)), ((), ())), preferred_element_type=F32
        )
        return jnp.dot(d, jnp.exp2(s).astype(BF), preferred_element_type=F32)

    half = Z * ROWS // 2
    forwards = [cols_in(0)]
    rows_in(0, Z // 2)
    acc[:, 0:half] = product(0, 0, 0, half)
    forwards.append(cols_in(1))
    acc[:, 0:half] += product(0, GROUP, 0, half)
    rows_in(Z // 2, Z)
    forwards.append(cols_in(2))
    acc[:, half:] = product(0, 0, half, half) + product(0, GROUP, half, half)
    forwards.append(cols_in(3))
    acc[...] += product(0, 2 * GROUP, 0, 2 * half)
    acc[...] += product(0, 3 * GROUP, 0, 2 * half)
    for g in range(PLANE // GROUP):
        forwards[g].wait_recv()
        acc[...] += product(1, g * GROUP, 0, 2 * half)

    homes = []
    for k in range(Z - 1, 0, -1):
        part[k] = acc[:, k * ROWS : (k + 1) * ROWS].astype(BF)
        copy = remote(part.at[k], part.at[Z + ring_back[k]], rs_s.at[k], rs_r.at[ring_back[k]], ring_id[k])
        copy.start()
        homes.append(copy)
    image = acc[:, 0:ROWS] + v_noise[...] * v_dir[...]
    for k in range(1, Z):
        remote(part.at[k], part.at[Z + k], rs_s.at[k], rs_r.at[k], ring_id[k]).wait_recv()
        image += part[Z + k].astype(F32)

    sums = pack(lane, total_lanes(v_dir[...] * image), 8, sums)
    sums = pack(lane, total_lanes(v_res[...] * image), 16, sums)
    sums = pack(lane, total_lanes(image * image), 24, sums)

    ar1[0] = sums
    firsts = [
        remote(ar1.at[0], ar1.at[column_back[k]], a1_s.at[k], a1_r.at[column_back[k]], column_id[k])
        for k in range(2 * Z - 1, 0, -1)
    ]
    for copy in firsts:
        copy.start()
    for k in range(1, 2 * Z):
        remote(ar1.at[0], ar1.at[k], a1_s.at[k], a1_r.at[k], column_id[k]).wait_recv()
    ar2[0] = jnp.sum(ar1[...], axis=0)
    seconds = [
        remote(ar2.at[0], ar2.at[plane_back[k]], a2_s.at[k], a2_r.at[plane_back[k]], plane_id[k])
        for k in range(PLANE - 1, 0, -1)
    ]
    for copy in seconds:
        copy.start()
    for k in range(1, PLANE):
        remote(ar2.at[0], ar2.at[k], a2_s.at[k], a2_r.at[k], plane_id[k]).wait_recv()
    total = jnp.sum(ar2[...], axis=0)

    alpha = total / pltpu.roll(total, 120, 1)
    change = alpha * (alpha * pltpu.roll(total, 104, 1) - 2.0 * pltpu.roll(total, 112, 1))
    beta = (total + change) / total
    for t in range(PROBES // 8):
        at8 = slice(8 * t, 8 * t + 8)
        o_alpha[at8] = jnp.broadcast_to(alpha[:, t : t + 1], (8, ROWS))
        o_beta[at8] = jnp.broadcast_to(beta[:, t : t + 1], (8, ROWS))
    o_image[...] = image

    for copy in rows + cols + forwards + homes + firsts + seconds:
        copy.wait_send()


def per_device(points, lengthscale, noise, solution, residual, direction):
    sems = pltpu.SemaphoreType.DMA
    out = jax.ShapeDtypeStruct((PROBES, ROWS), F32)
    hbm = pl.BlockSpec(memory_space=pltpu.HBM)
    vmem = pl.BlockSpec(memory_space=pltpu.VMEM)
    image, alpha, beta = pl.pallas_call(
        body,
        out_shape=(out, out, out),
        in_specs=[hbm] * 5,
        out_specs=(vmem, vmem, vmem),
        scratch_shapes=[
            pltpu.VMEM((FEATURES, ROWS), F32),
            pltpu.VMEM((1, FEATURES), F32),
            pltpu.VMEM((1, ROWS), F32),
            pltpu.VMEM((PROBES, ROWS), F32),
            pltpu.VMEM((PROBES, ROWS), F32),
            pltpu.VMEM((Z, 2 * FEATURES, ROWS), BF),
            pltpu.VMEM((2, PLANE, MSG, ROWS), BF),
            pltpu.VMEM((FEAT, Z * ROWS), BF),
            pltpu.VMEM((PROBES, Z * ROWS), F32),
            pltpu.VMEM((2 * Z, PROBES, ROWS), BF),
            pltpu.VMEM((2 * Z, 8, 128), F32),
            pltpu.VMEM((PLANE, 8, 128), F32),
            sems((5,)),
            sems((Z,)), sems((Z,)),
            sems((PLANE,)), sems((PLANE,)),
            sems((PLANE // GROUP,)), sems((PLANE // GROUP,)),
            sems((Z,)), sems((Z,)),
            sems((2 * Z,)), sems((2 * Z,)),
            sems((PLANE,)), sems((PLANE,)),
        ],
        compiler_params=pltpu.CompilerParams(
            collective_id=0, has_side_effects=True, vmem_limit_bytes=60 << 20
        ),
    )(
        points.T, lengthscale[None, :], noise[None, :], residual.T, direction.T
    )
    new_residual = residual - alpha.T * image.T
    return (
        solution + alpha.T * direction,
        new_residual,
        new_residual + beta.T * direction,
    )


def solution(mesh):
    placed = (P("blk", None), P(), P("blk"), P("blk", None), P("blk", None), P("blk", None))
    return jax.shard_map(
        per_device,
        mesh=mesh,
        in_specs=placed,
        out_specs=(P("blk", None), P("blk", None), P("blk", None)),
        check_vma=False,
    )
```

time: 47 us -> 39.3 us (0.84)
  local copies, waits for them, and re-layouts: 4.8 us -> 0.01 us
  Pallas kernels: 41.2 us -> 36.9 us
  other arithmetic: 0 us -> 1.46 us
    unnamed x15 -> x4, local copies, waits for them, and re-layouts: 4.8 us -> 0.01 us
    pallas_call x1, Pallas kernels: 41.2 us -> 36.9 us  [per_device(): pl.pallas_call(body, out_shape=(out, out, out), in_specs=[hbm] * 5, out_s...]
    add x0 -> x1, other arithmetic: none -> 1.46 us  [per_device(): new_residual + beta.T * direction]
where the time goes in v2:
time: 39.3 us; the launch traced here: 39.1 us
  Pallas kernels  36.9 us (94%)
  other arithmetic  1.46 us (4%)
  between operations  0.67 us (2%)
    pallas_call x1, Pallas kernels, per_device(): pl.pallas_call(body, out_shape=(out, out, out), in_specs=[hbm] * 5, out_s...  36.9 us
    add x1, other arithmetic, per_device(): new_residual + beta.T * direction  1.46 us

profile of v2, /device:TPU:1, one launch (start us, length us, event | category | flops | bytes accessed | tf_op | source)
XLA Modules:
  0.0 39.1 jit_solution(4927388741912769647)
XLA Ops:
  0.6 0.0 copy-start
  0.6 0.0 copy-start.1
  0.7 36.9 %shard_map.85 = (f32[64,128]{1,0:T(8,128)}, f32[64,128]{1,0:T(8,128)}, f32[64,128]{1,0:T(8,128)}) custom-call(f32[16,128]{1,0:T(8,128)} %bitcast.22, f32[1,16]{1,0:T(1,128)} %bitcast.23, f32[1,128]{1,0:T(1,128)} %bitcast.24, f32[64,128]{1,0:T(8,128)} %bitcast.21, f32[64,128]{1,0:T(8,128)} %bitcast.20), custom_call_target="tpu_custom_call" | custom-call | tf_op jit(solution)/shard_map/pallas_call | solution.py:243
  37.6 0.0 copy-done
  37.6 0.0 copy-done.1
  37.6 1.5 %fusion = (f32[128,64]{0,1:T(8,128)}, f32[128,64]{0,1:T(8,128)}, f32[128,64]{0,1:T(8,128)}) fusion(f32[128,64]{0,1:T(8,128)S(1)} %copy-done, f32[64,128]{1,0:T(8,128)} %get-tuple-element.8, f32[128,64]{0,1:T(8,128)S(1)} %copy-done.1, f32[64,128]{1,0:T(8,128)} %get-tuple-element.7, f32[64,128]{1,0:T(8,128)} %get-tuple-element.6, f32[128,64]{0,1:T(8,128)} %param.9), kind=kLoop, calls=%fused_computation.1 | loop fusion | flops 49152 | bytes 294912 | tf_op jit(solution)/shard_map/add | solution.py:279
Async XLA Ops:
  0.6 37.0 %copy-start = (f32[128,64]{0,1:T(8,128)S(1)}, f32[128,64]{0,1:T(8,128)}, u32[]{:S(2)}) copy-start(f32[128,64]{0,1:T(8,128)} %param.11) | copy-start | bytes 98308
  0.6 37.0 %copy-start.1 = (f32[128,64]{0,1:T(8,128)S(1)}, f32[128,64]{0,1:T(8,128)}, u32[]{:S(2)}) copy-start(f32[128,64]{0,1:T(8,128)} %param.10) | copy-start | bytes 98308

commit v3 on v2

--- a/solution.py
+++ b/solution.py
@@ -55,9 +55,9 @@
 
 
 def body(
-    pts, ls, noise, res, dirn,
-    o_image, o_alpha, o_beta,
-    v_pts, v_ls, v_noise, v_res, v_dir,
+    pts, ls, noise, sol, res, dirn,
+    v_sol, v_res, o_move, o_drop, o_push,
+    v_pts, v_ls, v_noise, v_dir,
     rowbuf, colbuf, feat, acc, part, ar1, ar2,
     in_sem, row_s, row_r, col_s, col_r, sib_s, sib_r, rs_s, rs_r, a1_s, a1_r, a2_s, a2_r,
 ):
@@ -93,17 +93,17 @@
             src_ref=src, dst_ref=dst, send_sem=s, recv_sem=r, device_id=(dev,), device_id_type=MESH
         )
 
+    barrier = pltpu.get_barrier_semaphore()
+    for dev in ring_id[:0:-1] + plane_id[:0:-1] + [sibling]:
+        pl.semaphore_signal(barrier, inc=1, device_id=(dev,), device_id_type=MESH)
     loads = [
         pltpu.make_async_copy(src, dst, in_sem.at[i])
         for i, (src, dst) in enumerate(
-            ((pts, v_pts), (ls, v_ls), (dirn, v_dir), (res, v_res), (noise, v_noise))
+            ((pts, v_pts), (ls, v_ls), (dirn, v_dir), (res, v_res), (noise, v_noise), (sol, v_sol))
         )
     ]
     for load in loads:
         load.start()
-    barrier = pltpu.get_barrier_semaphore()
-    for dev in ring_id[:0:-1] + plane_id[:0:-1] + [sibling]:
-        pl.semaphore_signal(barrier, inc=1, device_id=(dev,), device_id_type=MESH)
 
     loads[0].wait()
     loads[1].wait()
@@ -130,7 +130,7 @@
         remote(
             colbuf.at[0, 0], colbuf.at[0, plane_back[k]], col_s.at[k], col_r.at[plane_back[k]], plane_id[k]
         )
-        for k in range(PLANE - 1, 0, -1)
+        for k in range(1, PLANE)
     ]
     for copy in rows + cols:
         copy.start()
@@ -140,10 +140,10 @@
     lane = lax.broadcasted_iota(jnp.int32, (8, 128), 1)
     sums = pack(lane, total_lanes(v_res[...] * v_res[...]), 0, jnp.zeros((8, 128), F32))
 
-    def rows_in(first, last):
-        for k in range(max(first, 1), last):
+    def rows_in():
+        for k in range(1, Z):
             remote(rowbuf.at[0], rowbuf.at[k], row_s.at[k], row_r.at[k], ring_id[k]).wait_recv()
-        for k in range(first, last):
+        for k in range(Z):
             feat[:, k * ROWS : (k + 1) * ROWS] = row_features(
                 rowbuf[k, 0:FEATURES], rowbuf[k, FEATURES : 2 * FEATURES]
             )
@@ -156,43 +156,45 @@
         copy.start()
         return copy
 
-    def product(half, first, rows_at, rows_n):
-        blocks = range(first, first + GROUP)
-        b = jnp.concatenate(
-            [
-                col_features(colbuf[half, j, 0:FEATURES], colbuf[half, j, FEATURES : 2 * FEATURES])
-                for j in blocks
-            ],
-            axis=1,
-        )
-        d = jnp.concatenate([colbuf[half, j, 2 * FEATURES : MSG] for j in blocks], axis=1)
-        s = lax.dot_general(
-            b, feat[:, rows_at : rows_at + rows_n], (((0,), (0,)), ((), ())), preferred_element_type=F32
-        )
+    def columns_of(groups):
+        blocks = [(core, j) for core, g in groups for j in range(g * GROUP, (g + 1) * GROUP)]
+        b = [
+            col_features(colbuf[core, j, 0:FEATURES], colbuf[core, j, FEATURES : 2 * FEATURES])
+            for core, j in blocks
+        ]
+        d = [colbuf[core, j, 2 * FEATURES : MSG] for core, j in blocks]
+        return jnp.concatenate(b, axis=1).T, jnp.concatenate(d, axis=1)
+
+    def product(b, d, rows_of=slice(None)):
+        s = jnp.dot(b, feat[:, rows_of], preferred_element_type=F32)
         return jnp.dot(d, jnp.exp2(s).astype(BF), preferred_element_type=F32)
 
-    half = Z * ROWS // 2
     forwards = [cols_in(0)]
-    rows_in(0, Z // 2)
-    acc[:, 0:half] = product(0, 0, 0, half)
+    rows_in()
     forwards.append(cols_in(1))
-    acc[:, 0:half] += product(0, GROUP, 0, half)
-    rows_in(Z // 2, Z)
+    acc[...] = product(*columns_of(((0, 0), (0, 1))))
     forwards.append(cols_in(2))
-    acc[:, half:] = product(0, 0, half, half) + product(0, GROUP, half, half)
+    forwards[0].wait_recv()
+    acc[...] += product(*columns_of(((0, 2), (1, 0))))
     forwards.append(cols_in(3))
-    acc[...] += product(0, 2 * GROUP, 0, 2 * half)
-    acc[...] += product(0, 3 * GROUP, 0, 2 * half)
-    for g in range(PLANE // GROUP):
-        forwards[g].wait_recv()
-        acc[...] += product(1, g * GROUP, 0, 2 * half)
-
+    forwards[1].wait_recv()
+    forwards[2].wait_recv()
+    acc[...] += product(*columns_of(((1, 1), (1, 2), (0, 3))))
+    forwards[3].wait_recv()
+    last = ((1, 3),)
+
+    b, d = columns_of(last)
     homes = []
-    for k in range(Z - 1, 0, -1):
-        part[k] = acc[:, k * ROWS : (k + 1) * ROWS].astype(BF)
-        copy = remote(part.at[k], part.at[Z + ring_back[k]], rs_s.at[k], rs_r.at[ring_back[k]], ring_id[k])
-        copy.start()
-        homes.append(copy)
+    for first in (Z // 2, 0):
+        rows_of = slice(first * ROWS, (first + Z // 2) * ROWS)
+        acc[:, rows_of] += product(b, d, rows_of)
+        for k in range(first + Z // 2 - 1, max(first, 1) - 1, -1):
+            part[k] = acc[:, k * ROWS : (k + 1) * ROWS].astype(BF)
+            copy = remote(part.at[k], part.at[Z + ring_back[k]], rs_s.at[k], rs_r.at[ring_back[k]], ring_id[k])
+            copy.start()
+            homes.append(copy)
+    for copy in rows + cols + forwards:
+        copy.wait_send()
     image = acc[:, 0:ROWS] + v_noise[...] * v_dir[...]
     for k in range(1, Z):
         remote(part.at[k], part.at[Z + k], rs_s.at[k], rs_r.at[k], ring_id[k]).wait_recv()
@@ -209,6 +211,8 @@
     ]
     for copy in firsts:
         copy.start()
+    for copy in homes:
+        copy.wait_send()
     for k in range(1, 2 * Z):
         remote(ar1.at[0], ar1.at[k], a1_s.at[k], a1_r.at[k], column_id[k]).wait_recv()
     ar2[0] = jnp.sum(ar1[...], axis=0)
@@ -218,6 +222,8 @@
     ]
     for copy in seconds:
         copy.start()
+    for copy in firsts:
+        copy.wait_send()
     for k in range(1, PLANE):
         remote(ar2.at[0], ar2.at[k], a2_s.at[k], a2_r.at[k], plane_id[k]).wait_recv()
     total = jnp.sum(ar2[...], axis=0)
@@ -227,29 +233,29 @@
     beta = (total + change) / total
     for t in range(PROBES // 8):
         at8 = slice(8 * t, 8 * t + 8)
-        o_alpha[at8] = jnp.broadcast_to(alpha[:, t : t + 1], (8, ROWS))
-        o_beta[at8] = jnp.broadcast_to(beta[:, t : t + 1], (8, ROWS))
-    o_image[...] = image
-
-    for copy in rows + cols + forwards + homes + firsts + seconds:
+        a = alpha[:, t : t + 1]
+        o_move[at8] = a * v_dir[at8]
+        o_drop[at8] = a * image[at8]
+        o_push[at8] = beta[:, t : t + 1] * v_dir[at8]
+
+    for copy in seconds:
         copy.wait_send()
 
 
 def per_device(points, lengthscale, noise, solution, residual, direction):
     sems = pltpu.SemaphoreType.DMA
-    out = jax.ShapeDtypeStruct((PROBES, ROWS), F32)
+    out = pltpu.VMEM((PROBES, ROWS), F32)
     hbm = pl.BlockSpec(memory_space=pltpu.HBM)
     vmem = pl.BlockSpec(memory_space=pltpu.VMEM)
-    image, alpha, beta = pl.pallas_call(
+    sol, res, move, drop, push = pl.pallas_call(
         body,
-        out_shape=(out, out, out),
-        in_specs=[hbm] * 5,
-        out_specs=(vmem, vmem, vmem),
+        out_shape=(out,) * 5,
+        in_specs=[hbm] * 6,
+        out_specs=(vmem,) * 5,
         scratch_shapes=[
             pltpu.VMEM((FEATURES, ROWS), F32),
             pltpu.VMEM((1, FEATURES), F32),
             pltpu.VMEM((1, ROWS), F32),
-            pltpu.VMEM((PROBES, ROWS), F32),
             pltpu.VMEM((PROBES, ROWS), F32),
             pltpu.VMEM((Z, 2 * FEATURES, ROWS), BF),
             pltpu.VMEM((2, PLANE, MSG, ROWS), BF),
@@ -258,7 +264,7 @@
             pltpu.VMEM((2 * Z, PROBES, ROWS), BF),
             pltpu.VMEM((2 * Z, 8, 128), F32),
             pltpu.VMEM((PLANE, 8, 128), F32),
-            sems((5,)),
+            sems((6,)),
             sems((Z,)), sems((Z,)),
             sems((PLANE,)), sems((PLANE,)),
             sems((PLANE // GROUP,)), sems((PLANE // GROUP,)),
@@ -267,17 +273,16 @@
             sems((PLANE,)), sems((PLANE,)),
         ],
         compiler_params=pltpu.CompilerParams(
-            collective_id=0, has_side_effects=True, vmem_limit_bytes=60 << 20
+            collective_id=0, has_side_effects=True, vmem_limit_bytes=32 << 20
         ),
     )(
-        points.T, lengthscale[None, :], noise[None, :], residual.T, direction.T
+        *(
+            pltpu.with_memory_space_constraint(v, pltpu.HBM)
+            for v in (points.T, lengthscale[None, :], noise[None, :], solution.T, residual.T, direction.T)
+        )
     )
-    new_residual = residual - alpha.T * image.T
-    return (
-        solution + alpha.T * direction,
-        new_residual,
-        new_residual + beta.T * direction,
-    )
+    new_residual = res - drop
+    return (sol + move).T, new_residual.T, (new_residual + push).T
 
 
 def solution(mesh):

time: 39.3 us -> 37.6 us (0.957)
  other arithmetic: 1.46 us -> 0.64 us
  Pallas kernels: 36.9 us -> 36.1 us
    add x1 -> x0, other arithmetic: 1.46 us -> none  [per_device(): new_residual + beta.T * direction]
    pallas_call x1, Pallas kernels: 36.9 us -> 36.1 us  [per_device(): pl.pallas_call(body, out_shape=(out,) * 5, in_specs=[hbm] * 6, out_specs=...]
    transpose x0 -> x1, other arithmetic: none -> 0.64 us  [per_device(): return ((sol + move).T, new_residual.T, (new_residual + push).T)]
where the time goes in v3:
time: 37.6 us; the launch traced here: 37.4 us
  Pallas kernels  36.1 us (96%)
  other arithmetic  0.64 us (2%)
  between operations  0.64 us (2%)
    pallas_call x1, Pallas kernels, per_device(): pl.pallas_call(body, out_shape=(out,) * 5, in_specs=[hbm] * 6, out_specs=...  36.1 us

profile of v3, /device:TPU:1, one launch (start us, length us, event | category | flops | bytes accessed | tf_op | source)
XLA Modules:
  0.0 37.4 jit_solution(632880293181076898)
XLA Ops:
  0.6 36.1 %shard_map.85 = (f32[64,128]{1,0:T(8,128)S(1)}, f32[64,128]{1,0:T(8,128)S(1)}, f32[64,128]{1,0:T(8,128)S(1)}, f32[64,128]{1,0:T(8,128)S(1)}, f32[64,128]{1,0:T(8,128)S(1)}) custom-call(f32[16,128]{1,0:T(8,128)} %bitcast.15, f32[1,16]{1,0:T(1,128)} %bitcast.16, f32[1,128]{1,0:T(1,128)} %bitcast.17, f32[64,128]{1,0:T(8,128)} %bitcast.12, f32[64,128]{1,0:T(8,128)} %bitcast.13, ...), custom_call_target="tpu_custom_call" | custom-call | tf_op jit(solution)/shard_map/pallas_call | solution.py:250
  36.8 0.6 %add_bitcast_fusion = (f32[128,64]{0,1:T(8,128)}, f32[128,64]{0,1:T(8,128)}, f32[128,64]{0,1:T(8,128)}) fusion(f32[64,128]{1,0:T(8,128)S(1)} %get-tuple-element.12, f32[64,128]{1,0:T(8,128)S(1)} %get-tuple-element.10, f32[64,128]{1,0:T(8,128)S(1)} %get-tuple-element.11, f32[64,128]{1,0:T(8,128)S(1)} %get-tuple-element.8, f32[64,128]{1,0:T(8,128)S(1)} %get-tuple-element.9), kind=kLoop, calls=%fused_computation | loop fusion | flops 24576 | bytes 262144 | tf_op jit(solution)/shard_map/transpose | solution.py:285

commit v4 on v3

--- a/solution.py
+++ b/solution.py
@@ -123,17 +123,26 @@
 
     pl.semaphore_wait(barrier, PLANE + Z - 1)
     rows = [
-        remote(rowbuf.at[0], rowbuf.at[ring_back[k]], row_s.at[k], row_r.at[ring_back[k]], ring_id[k])
+        remote(rowbuf.at[0], rowbuf.at[ring_back[k]], row_s.at[0], row_r.at[0], ring_id[k])
         for k in range(Z - 1, 0, -1)
     ]
     cols = [
         remote(
-            colbuf.at[0, 0], colbuf.at[0, plane_back[k]], col_s.at[k], col_r.at[plane_back[k]], plane_id[k]
+            colbuf.at[0, 0],
+            colbuf.at[0, plane_back[k]],
+            col_s.at[0],
+            col_r.at[plane_back[k] // GROUP],
+            plane_id[k],
         )
         for k in range(1, PLANE)
     ]
-    for copy in rows + cols:
+    for copy in cols[:4] + rows + cols[4:]:
         copy.start()
+
+    others = pl.ds(1, Z - 1)
+    all_rows = remote(rowbuf.at[others], rowbuf.at[others], row_s.at[0], row_r.at[0], sibling)
+    others = pl.ds(1, PLANE - 1)
+    all_cols = remote(colbuf.at[0, others], colbuf.at[0, others], col_s.at[0], col_r.at[0], sibling)
 
     for load in loads[3:]:
         load.wait()
@@ -141,16 +150,16 @@
     sums = pack(lane, total_lanes(v_res[...] * v_res[...]), 0, jnp.zeros((8, 128), F32))
 
     def rows_in():
-        for k in range(1, Z):
-            remote(rowbuf.at[0], rowbuf.at[k], row_s.at[k], row_r.at[k], ring_id[k]).wait_recv()
+        all_rows.wait_recv()
         for k in range(Z):
             feat[:, k * ROWS : (k + 1) * ROWS] = row_features(
                 rowbuf[k, 0:FEATURES], rowbuf[k, FEATURES : 2 * FEATURES]
             )
 
     def cols_in(g):
-        for k in range(max(g * GROUP, 1), (g + 1) * GROUP):
-            remote(colbuf.at[0, 0], colbuf.at[0, k], col_s.at[k], col_r.at[k], plane_id[k]).wait_recv()
+        first = max(g * GROUP, 1)
+        came = colbuf.at[0, pl.ds(first, (g + 1) * GROUP - first)]
+        remote(came, came, col_s.at[0], col_r.at[g], sibling).wait_recv()
         here = pl.ds(g * GROUP, GROUP)
         copy = remote(colbuf.at[0, here], colbuf.at[1, here], sib_s.at[g], sib_r.at[g], sibling)
         copy.start()
@@ -171,33 +180,35 @@
 
     forwards = [cols_in(0)]
     rows_in()
+    acc[...] = product(*columns_of(((0, 0),)))
     forwards.append(cols_in(1))
-    acc[...] = product(*columns_of(((0, 0), (0, 1))))
+    forwards[0].wait_recv()
+    acc[...] += product(*columns_of(((0, 1), (1, 0))))
     forwards.append(cols_in(2))
-    forwards[0].wait_recv()
-    acc[...] += product(*columns_of(((0, 2), (1, 0))))
+    forwards[1].wait_recv()
+    acc[...] += product(*columns_of(((0, 2), (1, 1))))
     forwards.append(cols_in(3))
-    forwards[1].wait_recv()
     forwards[2].wait_recv()
-    acc[...] += product(*columns_of(((1, 1), (1, 2), (0, 3))))
+    acc[...] += product(*columns_of(((1, 2), (0, 3))))
     forwards[3].wait_recv()
     last = ((1, 3),)
 
     b, d = columns_of(last)
-    homes = []
     for first in (Z // 2, 0):
         rows_of = slice(first * ROWS, (first + Z // 2) * ROWS)
         acc[:, rows_of] += product(b, d, rows_of)
         for k in range(first + Z // 2 - 1, max(first, 1) - 1, -1):
             part[k] = acc[:, k * ROWS : (k + 1) * ROWS].astype(BF)
-            copy = remote(part.at[k], part.at[Z + ring_back[k]], rs_s.at[k], rs_r.at[ring_back[k]], ring_id[k])
+            copy = remote(part.at[k], part.at[Z + ring_back[k]], rs_s.at[0], rs_r.at[0], ring_id[k])
             copy.start()
-            homes.append(copy)
-    for copy in rows + cols + forwards:
+    for copy in [all_rows, all_cols] + forwards:
         copy.wait_send()
     image = acc[:, 0:ROWS] + v_noise[...] * v_dir[...]
+    home = remote(
+        part.at[pl.ds(1, Z - 1)], part.at[pl.ds(Z + 1, Z - 1)], rs_s.at[0], rs_r.at[0], sibling
+    )
+    home.wait_recv()
     for k in range(1, Z):
-        remote(part.at[k], part.at[Z + k], rs_s.at[k], rs_r.at[k], ring_id[k]).wait_recv()
         image += part[Z + k].astype(F32)
 
     sums = pack(lane, total_lanes(v_dir[...] * image), 8, sums)
@@ -206,26 +217,26 @@
 
     ar1[0] = sums
     firsts = [
-        remote(ar1.at[0], ar1.at[column_back[k]], a1_s.at[k], a1_r.at[column_back[k]], column_id[k])
+        remote(ar1.at[0], ar1.at[column_back[k]], a1_s.at[0], a1_r.at[0], column_id[k])
         for k in range(2 * Z - 1, 0, -1)
     ]
     for copy in firsts:
         copy.start()
-    for copy in homes:
-        copy.wait_send()
-    for k in range(1, 2 * Z):
-        remote(ar1.at[0], ar1.at[k], a1_s.at[k], a1_r.at[k], column_id[k]).wait_recv()
+    home.wait_send()
+    others = pl.ds(1, 2 * Z - 1)
+    arrived = remote(ar1.at[others], ar1.at[others], a1_s.at[0], a1_r.at[0], sibling)
+    arrived.wait_recv()
     ar2[0] = jnp.sum(ar1[...], axis=0)
     seconds = [
-        remote(ar2.at[0], ar2.at[plane_back[k]], a2_s.at[k], a2_r.at[plane_back[k]], plane_id[k])
+        remote(ar2.at[0], ar2.at[plane_back[k]], a2_s.at[0], a2_r.at[0], plane_id[k])
         for k in range(PLANE - 1, 0, -1)
     ]
     for copy in seconds:
         copy.start()
-    for copy in firsts:
-        copy.wait_send()
-    for k in range(1, PLANE):
-        remote(ar2.at[0], ar2.at[k], a2_s.at[k], a2_r.at[k], plane_id[k]).wait_recv()
+    arrived.wait_send()
+    others = pl.ds(1, PLANE - 1)
+    finished = remote(ar2.at[others], ar2.at[others], a2_s.at[0], a2_r.at[0], sibling)
+    finished.wait_recv()
     total = jnp.sum(ar2[...], axis=0)
 
     alpha = total / pltpu.roll(total, 120, 1)
@@ -238,8 +249,7 @@
         o_drop[at8] = a * image[at8]
         o_push[at8] = beta[:, t : t + 1] * v_dir[at8]
 
-    for copy in seconds:
-        copy.wait_send()
+    finished.wait_send()
 
 
 def per_device(points, lengthscale, noise, solution, residual, direction):
@@ -265,12 +275,12 @@
             pltpu.VMEM((2 * Z, 8, 128), F32),
             pltpu.VMEM((PLANE, 8, 128), F32),
             sems((6,)),
-            sems((Z,)), sems((Z,)),
-            sems((PLANE,)), sems((PLANE,)),
+            sems((1,)), sems((1,)),
+            sems((1,)), sems((PLANE // GROUP,)),
             sems((PLANE // GROUP,)), sems((PLANE // GROUP,)),
-            sems((Z,)), sems((Z,)),
-            sems((2 * Z,)), sems((2 * Z,)),
-            sems((PLANE,)), sems((PLANE,)),
+            sems((1,)), sems((1,)),
+            sems((1,)), sems((1,)),
+            sems((1,)), sems((1,)),
         ],
         compiler_params=pltpu.CompilerParams(
             collective_id=0, has_side_effects=True, vmem_limit_bytes=32 << 20

time: 37.6 us -> 36.4 us (0.968)
  Pallas kernels: 36.1 us -> 34.9 us
    pallas_call x1, Pallas kernels: 36.1 us -> 34.9 us  [per_device(): pl.pallas_call(body, out_shape=(out,) * 5, in_specs=[hbm] * 6, out_specs=...]
where the time goes in v4:
time: 36.4 us; the launch traced here: 36.2 us
  Pallas kernels  34.9 us (96%)
  other arithmetic  0.64 us (2%)
  between operations  0.64 us (2%)
    pallas_call x1, Pallas kernels, per_device(): pl.pallas_call(body, out_shape=(out,) * 5, in_specs=[hbm] * 6, out_specs=...  34.9 us

profile of v4, /device:TPU:1, one launch (start us, length us, event | category | flops | bytes accessed | tf_op | source)
XLA Modules:
  0.0 36.2 jit_solution(13457368715922718942)
XLA Ops:
  0.6 34.9 %shard_map.85 = (f32[64,128]{1,0:T(8,128)S(1)}, f32[64,128]{1,0:T(8,128)S(1)}, f32[64,128]{1,0:T(8,128)S(1)}, f32[64,128]{1,0:T(8,128)S(1)}, f32[64,128]{1,0:T(8,128)S(1)}) custom-call(f32[16,128]{1,0:T(8,128)} %bitcast.15, f32[1,16]{1,0:T(1,128)} %bitcast.16, f32[1,128]{1,0:T(1,128)} %bitcast.17, f32[64,128]{1,0:T(8,128)} %bitcast.12, f32[64,128]{1,0:T(8,128)} %bitcast.13, ...), custom_call_target="tpu_custom_call" | custom-call | tf_op jit(solution)/shard_map/pallas_call | solution.py:260
  35.6 0.6 %add_bitcast_fusion = (f32[128,64]{0,1:T(8,128)}, f32[128,64]{0,1:T(8,128)}, f32[128,64]{0,1:T(8,128)}) fusion(f32[64,128]{1,0:T(8,128)S(1)} %get-tuple-element.12, f32[64,128]{1,0:T(8,128)S(1)} %get-tuple-element.10, f32[64,128]{1,0:T(8,128)S(1)} %get-tuple-element.11, f32[64,128]{1,0:T(8,128)S(1)} %get-tuple-element.8, f32[64,128]{1,0:T(8,128)S(1)} %get-tuple-element.9), kind=kLoop, calls=%fused_computation | loop fusion | flops 24576 | bytes 262144 | tf_op jit(solution)/shard_map/transpose | solution.py:295

commit v5 on v4

--- a/solution.py
+++ b/solution.py
@@ -48,10 +48,8 @@
     return jnp.sum(v, axis=1, keepdims=True)
 
 
-def pack(lane, cols, first, out):
-    for t in range(PROBES // 8):
-        out = jnp.where(lane == first + t, cols[8 * t : 8 * t + 8], out)
-    return out
+def row_sums(upper, lower):
+    return jnp.sum(jnp.concatenate([upper, lower], axis=0).T, axis=0, keepdims=True)
 
 
 def body(
@@ -59,7 +57,7 @@
     v_sol, v_res, o_move, o_drop, o_push,
     v_pts, v_ls, v_noise, v_dir,
     rowbuf, colbuf, feat, acc, part, ar1, ar2,
-    in_sem, row_s, row_r, col_s, col_r, sib_s, sib_r, rs_s, rs_r, a1_s, a1_r, a2_s, a2_r,
+    in_sem, out_s, row_r, col_r, sib_r, rs_r, a1_r, a2_r,
 ):
     me = lax.axis_index("blk")
     c = lax.rem(me, 2)
@@ -97,12 +95,12 @@
     for dev in ring_id[:0:-1] + plane_id[:0:-1] + [sibling]:
         pl.semaphore_signal(barrier, inc=1, device_id=(dev,), device_id_type=MESH)
     loads = [
-        pltpu.make_async_copy(src, dst, in_sem.at[i])
+        pltpu.make_async_copy(src, dst, in_sem.at[i % 3])
         for i, (src, dst) in enumerate(
             ((pts, v_pts), (ls, v_ls), (dirn, v_dir), (res, v_res), (noise, v_noise), (sol, v_sol))
         )
     ]
-    for load in loads:
+    for load in loads[:3]:
         load.start()
 
     loads[0].wait()
@@ -119,18 +117,20 @@
     colbuf[0, 0, 0:FEATURES] = hi
     colbuf[0, 0, FEATURES : 2 * FEATURES] = lo
     loads[2].wait()
+    for load in loads[3:]:
+        load.start()
     colbuf[0, 0, 2 * FEATURES : MSG] = v_dir[...].astype(BF)
 
     pl.semaphore_wait(barrier, PLANE + Z - 1)
     rows = [
-        remote(rowbuf.at[0], rowbuf.at[ring_back[k]], row_s.at[0], row_r.at[0], ring_id[k])
+        remote(rowbuf.at[0], rowbuf.at[ring_back[k]], out_s.at[0], row_r.at[0], ring_id[k])
         for k in range(Z - 1, 0, -1)
     ]
     cols = [
         remote(
             colbuf.at[0, 0],
             colbuf.at[0, plane_back[k]],
-            col_s.at[0],
+            out_s.at[1],
             col_r.at[plane_back[k] // GROUP],
             plane_id[k],
         )
@@ -140,14 +140,12 @@
         copy.start()
 
     others = pl.ds(1, Z - 1)
-    all_rows = remote(rowbuf.at[others], rowbuf.at[others], row_s.at[0], row_r.at[0], sibling)
+    all_rows = remote(rowbuf.at[others], rowbuf.at[others], out_s.at[0], row_r.at[0], sibling)
     others = pl.ds(1, PLANE - 1)
-    all_cols = remote(colbuf.at[0, others], colbuf.at[0, others], col_s.at[0], col_r.at[0], sibling)
+    all_cols = remote(colbuf.at[0, others], colbuf.at[0, others], out_s.at[1], col_r.at[0], sibling)
 
     for load in loads[3:]:
         load.wait()
-    lane = lax.broadcasted_iota(jnp.int32, (8, 128), 1)
-    sums = pack(lane, total_lanes(v_res[...] * v_res[...]), 0, jnp.zeros((8, 128), F32))
 
     def rows_in():
         all_rows.wait_recv()
@@ -159,9 +157,9 @@
     def cols_in(g):
         first = max(g * GROUP, 1)
         came = colbuf.at[0, pl.ds(first, (g + 1) * GROUP - first)]
-        remote(came, came, col_s.at[0], col_r.at[g], sibling).wait_recv()
+        remote(came, came, out_s.at[1], col_r.at[g], sibling).wait_recv()
         here = pl.ds(g * GROUP, GROUP)
-        copy = remote(colbuf.at[0, here], colbuf.at[1, here], sib_s.at[g], sib_r.at[g], sibling)
+        copy = remote(colbuf.at[0, here], colbuf.at[1, here], out_s.at[2], sib_r.at[g], sibling)
         copy.start()
         return copy
 
@@ -185,13 +183,12 @@
     forwards[0].wait_recv()
     acc[...] += product(*columns_of(((0, 1), (1, 0))))
     forwards.append(cols_in(2))
+    forwards.append(cols_in(3))
     forwards[1].wait_recv()
-    acc[...] += product(*columns_of(((0, 2), (1, 1))))
-    forwards.append(cols_in(3))
+    acc[...] += product(*columns_of(((0, 2), (0, 3), (1, 1))))
     forwards[2].wait_recv()
-    acc[...] += product(*columns_of(((1, 2), (0, 3))))
     forwards[3].wait_recv()
-    last = ((1, 3),)
+    last = ((1, 2), (1, 3))
 
     b, d = columns_of(last)
     for first in (Z // 2, 0):
@@ -199,55 +196,54 @@
         acc[:, rows_of] += product(b, d, rows_of)
         for k in range(first + Z // 2 - 1, max(first, 1) - 1, -1):
             part[k] = acc[:, k * ROWS : (k + 1) * ROWS].astype(BF)
-            copy = remote(part.at[k], part.at[Z + ring_back[k]], rs_s.at[0], rs_r.at[0], ring_id[k])
+            copy = remote(part.at[k], part.at[Z + ring_back[k]], out_s.at[3], rs_r.at[0], ring_id[k])
             copy.start()
-    for copy in [all_rows, all_cols] + forwards:
+    every = remote(colbuf.at[0], colbuf.at[1], out_s.at[2], sib_r.at[0], sibling)
+    for copy in (all_rows, all_cols, every):
         copy.wait_send()
     image = acc[:, 0:ROWS] + v_noise[...] * v_dir[...]
     home = remote(
-        part.at[pl.ds(1, Z - 1)], part.at[pl.ds(Z + 1, Z - 1)], rs_s.at[0], rs_r.at[0], sibling
+        part.at[pl.ds(1, Z - 1)], part.at[pl.ds(Z + 1, Z - 1)], out_s.at[3], rs_r.at[0], sibling
     )
     home.wait_recv()
     for k in range(1, Z):
         image += part[Z + k].astype(F32)
 
-    sums = pack(lane, total_lanes(v_dir[...] * image), 8, sums)
-    sums = pack(lane, total_lanes(v_res[...] * image), 16, sums)
-    sums = pack(lane, total_lanes(image * image), 24, sums)
-
-    ar1[0] = sums
+    ar1[0, 0:1] = row_sums(v_res[...] * v_res[...], v_dir[...] * image)
+    ar1[0, 1:2] = row_sums(v_res[...] * image, image * image)
     firsts = [
-        remote(ar1.at[0], ar1.at[column_back[k]], a1_s.at[0], a1_r.at[0], column_id[k])
+        remote(ar1.at[0], ar1.at[column_back[k]], out_s.at[0], a1_r.at[0], column_id[k])
         for k in range(2 * Z - 1, 0, -1)
     ]
     for copy in firsts:
         copy.start()
     home.wait_send()
     others = pl.ds(1, 2 * Z - 1)
-    arrived = remote(ar1.at[others], ar1.at[others], a1_s.at[0], a1_r.at[0], sibling)
+    arrived = remote(ar1.at[others], ar1.at[others], out_s.at[0], a1_r.at[0], sibling)
     arrived.wait_recv()
     ar2[0] = jnp.sum(ar1[...], axis=0)
     seconds = [
-        remote(ar2.at[0], ar2.at[plane_back[k]], a2_s.at[0], a2_r.at[0], plane_id[k])
+        remote(ar2.at[0], ar2.at[plane_back[k]], out_s.at[1], a2_r.at[0], plane_id[k])
         for k in range(PLANE - 1, 0, -1)
     ]
     for copy in seconds:
         copy.start()
     arrived.wait_send()
     others = pl.ds(1, PLANE - 1)
-    finished = remote(ar2.at[others], ar2.at[others], a2_s.at[0], a2_r.at[0], sibling)
+    finished = remote(ar2.at[others], ar2.at[others], out_s.at[1], a2_r.at[0], sibling)
     finished.wait_recv()
     total = jnp.sum(ar2[...], axis=0)
 
-    alpha = total / pltpu.roll(total, 120, 1)
-    change = alpha * (alpha * pltpu.roll(total, 104, 1) - 2.0 * pltpu.roll(total, 112, 1))
-    beta = (total + change) / total
-    for t in range(PROBES // 8):
-        at8 = slice(8 * t, 8 * t + 8)
-        a = alpha[:, t : t + 1]
-        o_move[at8] = a * v_dir[at8]
-        o_drop[at8] = a * image[at8]
-        o_push[at8] = beta[:, t : t + 1] * v_dir[at8]
+    one, two = total[0:1], total[1:2]
+    alpha = one / pltpu.roll(one, PROBES, 1)
+    change = alpha * (alpha * pltpu.roll(two, PROBES, 1) - 2.0 * two)
+    beta = (one + change) / one
+    lane = lax.broadcasted_iota(jnp.int32, (1, 2 * PROBES), 1)
+    both = jnp.where(lane < PROBES, alpha, pltpu.roll(beta, PROBES, 1))
+    both = jnp.broadcast_to(both, (2 * PROBES, ROWS)).T
+    o_move[...] = both[0:PROBES] * v_dir[...]
+    o_drop[...] = both[0:PROBES] * image
+    o_push[...] = both[PROBES:] * v_dir[...]
 
     finished.wait_send()
 
@@ -272,15 +268,16 @@
             pltpu.VMEM((FEAT, Z * ROWS), BF),
             pltpu.VMEM((PROBES, Z * ROWS), F32),
             pltpu.VMEM((2 * Z, PROBES, ROWS), BF),
-            pltpu.VMEM((2 * Z, 8, 128), F32),
-            pltpu.VMEM((PLANE, 8, 128), F32),
-            sems((6,)),
-            sems((1,)), sems((1,)),
-            sems((1,)), sems((PLANE // GROUP,)),
-            sems((PLANE // GROUP,)), sems((PLANE // GROUP,)),
-            sems((1,)), sems((1,)),
-            sems((1,)), sems((1,)),
-            sems((1,)), sems((1,)),
+            pltpu.VMEM((2 * Z, 2, 2 * PROBES), F32),
+            pltpu.VMEM((PLANE, 2, 2 * PROBES), F32),
+            sems((3,)),
+            sems((4,)),
+            sems((1,)),
+            sems((PLANE // GROUP,)),
+            sems((PLANE // GROUP,)),
+            sems((1,)),
+            sems((1,)),
+            sems((1,)),
         ],
         compiler_params=pltpu.CompilerParams(
             collective_id=0, has_side_effects=True, vmem_limit_bytes=32 << 20

time: 36.4 us -> 35.9 us (0.986)
  Pallas kernels: 34.9 us -> 34.4 us
    pallas_call x1, Pallas kernels: 34.9 us -> 34.4 us  [per_device(): pl.pallas_call(body, out_shape=(out,) * 5, in_specs=[hbm] * 6, out_specs=...]
where the time goes in v5:
time: 35.9 us; the launch traced here: 35.7 us
  Pallas kernels  34.4 us (96%)
  other arithmetic  0.64 us (2%)
  between operations  0.64 us (2%)
    pallas_call x1, Pallas kernels, per_device(): pl.pallas_call(body, out_shape=(out,) * 5, in_specs=[hbm] * 6, out_specs=...  34.4 us

profile of v5, /device:TPU:1, one launch (start us, length us, event | category | flops | bytes accessed | tf_op | source)
XLA Modules:
  0.0 35.7 jit_solution(15353766389528316114)
XLA Ops:
  0.6 34.4 %shard_map.85 = (f32[64,128]{1,0:T(8,128)S(1)}, f32[64,128]{1,0:T(8,128)S(1)}, f32[64,128]{1,0:T(8,128)S(1)}, f32[64,128]{1,0:T(8,128)S(1)}, f32[64,128]{1,0:T(8,128)S(1)}) custom-call(f32[16,128]{1,0:T(8,128)} %bitcast.15, f32[1,16]{1,0:T(1,128)} %bitcast.16, f32[1,128]{1,0:T(1,128)} %bitcast.17, f32[64,128]{1,0:T(8,128)} %bitcast.12, f32[64,128]{1,0:T(8,128)} %bitcast.13, ...), custom_call_target="tpu_custom_call" | custom-call | tf_op jit(solution)/shard_map/pallas_call | solution.py:256
  35.1 0.6 %add_bitcast_fusion = (f32[128,64]{0,1:T(8,128)}, f32[128,64]{0,1:T(8,128)}, f32[128,64]{0,1:T(8,128)}) fusion(f32[64,128]{1,0:T(8,128)S(1)} %get-tuple-element.12, f32[64,128]{1,0:T(8,128)S(1)} %get-tuple-element.10, f32[64,128]{1,0:T(8,128)S(1)} %get-tuple-element.11, f32[64,128]{1,0:T(8,128)S(1)} %get-tuple-element.8, f32[64,128]{1,0:T(8,128)S(1)} %get-tuple-element.9), kind=kLoop, calls=%fused_computation | loop fusion | flops 24576 | bytes 262144 | tf_op jit(solution)/shard_map/transpose | solution.py:292

commit v6 on v5

--- a/solution.py
+++ b/solution.py
@@ -185,19 +185,25 @@
     forwards.append(cols_in(2))
     forwards.append(cols_in(3))
     forwards[1].wait_recv()
-    acc[...] += product(*columns_of(((0, 2), (0, 3), (1, 1))))
+    late = columns_of(((0, 2), (0, 3), (1, 1)))
+    far, near = slice(Z // 2 * ROWS, Z * ROWS), slice(0, Z // 2 * ROWS)
+    acc[:, far] += product(*late, far)
     forwards[2].wait_recv()
     forwards[3].wait_recv()
-    last = ((1, 2), (1, 3))
-
-    b, d = columns_of(last)
-    for first in (Z // 2, 0):
-        rows_of = slice(first * ROWS, (first + Z // 2) * ROWS)
-        acc[:, rows_of] += product(b, d, rows_of)
-        for k in range(first + Z // 2 - 1, max(first, 1) - 1, -1):
+
+    last = columns_of(((1, 2), (1, 3)))
+
+    def send_home(first, end):
+        for k in range(end - 1, first - 1, -1):
             part[k] = acc[:, k * ROWS : (k + 1) * ROWS].astype(BF)
-            copy = remote(part.at[k], part.at[Z + ring_back[k]], out_s.at[3], rs_r.at[0], ring_id[k])
-            copy.start()
+            remote(
+                part.at[k], part.at[Z + ring_back[k]], out_s.at[3], rs_r.at[0], ring_id[k]
+            ).start()
+
+    acc[:, far] += product(*last, far)
+    send_home(Z // 2, Z)
+    acc[:, near] += product(*late, near) + product(*last, near)
+    send_home(1, Z // 2)
     every = remote(colbuf.at[0], colbuf.at[1], out_s.at[2], sib_r.at[0], sibling)
     for copy in (all_rows, all_cols, every):
         copy.wait_send()

time: 35.9 us -> 35.7 us (level)
  no operation moved by 1% of the time
where the time goes in v6:
time: 35.7 us; the launch traced here: 35.5 us
  Pallas kernels  34.2 us (96%)
  other arithmetic  0.64 us (2%)
  between operations  0.64 us (2%)
    pallas_call x1, Pallas kernels, per_device(): pl.pallas_call(body, out_shape=(out,) * 5, in_specs=[hbm] * 6, out_specs=...  34.2 us

profile of v6, /device:TPU:1, one launch (start us, length us, event | category | flops | bytes accessed | tf_op | source)
XLA Modules:
  0.0 35.5 jit_solution(14503575349827175517)
XLA Ops:
  0.6 34.2 %shard_map.85 = (f32[64,128]{1,0:T(8,128)S(1)}, f32[64,128]{1,0:T(8,128)S(1)}, f32[64,128]{1,0:T(8,128)S(1)}, f32[64,128]{1,0:T(8,128)S(1)}, f32[64,128]{1,0:T(8,128)S(1)}) custom-call(f32[16,128]{1,0:T(8,128)} %bitcast.15, f32[1,16]{1,0:T(1,128)} %bitcast.16, f32[1,128]{1,0:T(1,128)} %bitcast.17, f32[64,128]{1,0:T(8,128)} %bitcast.12, f32[64,128]{1,0:T(8,128)} %bitcast.13, ...), custom_call_target="tpu_custom_call" | custom-call | tf_op jit(solution)/shard_map/pallas_call | solution.py:262
  34.8 0.6 %add_bitcast_fusion = (f32[128,64]{0,1:T(8,128)}, f32[128,64]{0,1:T(8,128)}, f32[128,64]{0,1:T(8,128)}) fusion(f32[64,128]{1,0:T(8,128)S(1)} %get-tuple-element.12, f32[64,128]{1,0:T(8,128)S(1)} %get-tuple-element.10, f32[64,128]{1,0:T(8,128)S(1)} %get-tuple-element.11, f32[64,128]{1,0:T(8,128)S(1)} %get-tuple-element.8, f32[64,128]{1,0:T(8,128)S(1)} %get-tuple-element.9), kind=kLoop, calls=%fused_computation | loop fusion | flops 24576 | bytes 262144 | tf_op jit(solution)/shard_map/transpose | solution.py:298

commit v7 on v6

--- a/solution.py
+++ b/solution.py
@@ -15,7 +15,7 @@
 PLANE = X * Y
 MSG = 2 * FEATURES + PROBES
 FEAT = 5 * FEATURES
-GROUP = 4
+CUTS = (0, 5, 11, 16)
 ROOT_LOG2E = math.sqrt(math.log2(math.e))
 MESH = pl.DeviceIdType.MESH
 BF = jnp.bfloat16
@@ -131,7 +131,7 @@
             colbuf.at[0, 0],
             colbuf.at[0, plane_back[k]],
             out_s.at[1],
-            col_r.at[plane_back[k] // GROUP],
+            col_r.at[sum(plane_back[k] >= cut for cut in CUTS[1:])],
             plane_id[k],
         )
         for k in range(1, PLANE)
@@ -155,16 +155,16 @@
             )
 
     def cols_in(g):
-        first = max(g * GROUP, 1)
-        came = colbuf.at[0, pl.ds(first, (g + 1) * GROUP - first)]
+        first = max(CUTS[g], 1)
+        came = colbuf.at[0, pl.ds(first, CUTS[g + 1] - first)]
         remote(came, came, out_s.at[1], col_r.at[g], sibling).wait_recv()
-        here = pl.ds(g * GROUP, GROUP)
+        here = pl.ds(CUTS[g], CUTS[g + 1] - CUTS[g])
         copy = remote(colbuf.at[0, here], colbuf.at[1, here], out_s.at[2], sib_r.at[g], sibling)
         copy.start()
         return copy
 
     def columns_of(groups):
-        blocks = [(core, j) for core, g in groups for j in range(g * GROUP, (g + 1) * GROUP)]
+        blocks = [(core, j) for core, g in groups for j in range(CUTS[g], CUTS[g + 1])]
         b = [
             col_features(colbuf[core, j, 0:FEATURES], colbuf[core, j, FEATURES : 2 * FEATURES])
             for core, j in blocks
@@ -181,17 +181,15 @@
     acc[...] = product(*columns_of(((0, 0),)))
     forwards.append(cols_in(1))
     forwards[0].wait_recv()
-    acc[...] += product(*columns_of(((0, 1), (1, 0))))
+    acc[...] += product(*columns_of(((1, 0),)))
     forwards.append(cols_in(2))
-    forwards.append(cols_in(3))
-    forwards[1].wait_recv()
-    late = columns_of(((0, 2), (0, 3), (1, 1)))
+    late = columns_of(((0, 1), (0, 2)))
     far, near = slice(Z // 2 * ROWS, Z * ROWS), slice(0, Z // 2 * ROWS)
     acc[:, far] += product(*late, far)
+    forwards[1].wait_recv()
     forwards[2].wait_recv()
-    forwards[3].wait_recv()
-
-    last = columns_of(((1, 2), (1, 3)))
+
+    last = columns_of(((1, 1), (1, 2)))
 
     def send_home(first, end):
         for k in range(end - 1, first - 1, -1):
@@ -279,8 +277,8 @@
             sems((3,)),
             sems((4,)),
             sems((1,)),
-            sems((PLANE // GROUP,)),
-            sems((PLANE // GROUP,)),
+            sems((len(CUTS) - 1,)),
+            sems((len(CUTS) - 1,)),
             sems((1,)),
             sems((1,)),
             sems((1,)),

time: 35.7 us -> 35.6 us (level)
  no operation moved by 1% of the time
where the time goes in v7:
time: 35.6 us; the launch traced here: 35.4 us
  Pallas kernels  34.1 us (96%)
  other arithmetic  0.64 us (2%)
  between operations  0.64 us (2%)
    pallas_call x1, Pallas kernels, per_device(): pl.pallas_call(body, out_shape=(out,) * 5, in_specs=[hbm] * 6, out_specs=...  34.1 us

profile of v7, /device:TPU:1, one launch (start us, length us, event | category | flops | bytes accessed | tf_op | source)
XLA Modules:
  0.0 35.4 jit_solution(15271999409457282676)
XLA Ops:
  0.6 34.1 %shard_map.85 = (f32[64,128]{1,0:T(8,128)S(1)}, f32[64,128]{1,0:T(8,128)S(1)}, f32[64,128]{1,0:T(8,128)S(1)}, f32[64,128]{1,0:T(8,128)S(1)}, f32[64,128]{1,0:T(8,128)S(1)}) custom-call(f32[16,128]{1,0:T(8,128)} %bitcast.15, f32[1,16]{1,0:T(1,128)} %bitcast.16, f32[1,128]{1,0:T(1,128)} %bitcast.17, f32[64,128]{1,0:T(8,128)} %bitcast.12, f32[64,128]{1,0:T(8,128)} %bitcast.13, ...), custom_call_target="tpu_custom_call" | custom-call | tf_op jit(solution)/shard_map/pallas_call | solution.py:260
  34.7 0.6 %add_bitcast_fusion = (f32[128,64]{0,1:T(8,128)}, f32[128,64]{0,1:T(8,128)}, f32[128,64]{0,1:T(8,128)}) fusion(f32[64,128]{1,0:T(8,128)S(1)} %get-tuple-element.12, f32[64,128]{1,0:T(8,128)S(1)} %get-tuple-element.10, f32[64,128]{1,0:T(8,128)S(1)} %get-tuple-element.11, f32[64,128]{1,0:T(8,128)S(1)} %get-tuple-element.8, f32[64,128]{1,0:T(8,128)S(1)} %get-tuple-element.9), kind=kLoop, calls=%fused_computation | loop fusion | flops 24576 | bytes 262144 | tf_op jit(solution)/shard_map/transpose | solution.py:296
